TPU v7x, 512 devices: a whole 4x4x16 slice. The times are simulated.
512 devices in a mesh: row: 8 (over y, core), col: 8 (over x, z_hi), fsdp: 8 (over z_lo).
Axes of the slice: x: 4, y: 4, z: 16 (z_hi: 2, z_lo: 8; z = z_hi * 8 + z_lo), core: 2. Of those that a mesh axis runs over, the one named last changes fastest.
Arguments:
- master: float32 [8, 8, 192, 4096], P('row', 'col', 'fsdp'), may hold values from -6 to 6
- moment_one: float32 [8, 8, 192, 4096], P('row', 'col', 'fsdp'), may hold values from -3 to 3
- moment_two: float32 [8, 8, 192, 4096], P('row', 'col', 'fsdp'), may hold values from 0.01 to 1
- grads: bfloat16 [8, 8, 192, 4096], P('row', 'col', 'fsdp'), may hold values from -6 to 6
- counts: int32 [8, 8, 8], P('row', 'col'), may hold values from 1 to 4095
- step: int32 [1], replicated, may hold values from 1 to 15
Outputs:
- new_master: float32 [8, 8, 192, 4096], P('row', 'col', 'fsdp')
- new_moment_one: float32 [8, 8, 192, 4096], P('row', 'col', 'fsdp')
- new_moment_two: float32 [8, 8, 192, 4096], P('row', 'col', 'fsdp')
- replica_weights: bfloat16 [8, 8, 8, 192, 4096], P('row', 'col', 'fsdp')
All inputs are finite; a program needn't handle non-finite values.
Results may differ from a plain program's by a relative error of at most 0.001.
Values may be sent and summed in bfloat16 or wider, within the bound.
A program may use at most 64 MiB of HBM per device.

v0:
```python
import jax
import jax.numpy as jnp
from jax import lax
from jax.sharding import PartitionSpec as P


def passed_along(block, axis, distance):
    devices = range(lax.axis_size(axis))
    route = [((i - distance) % len(devices), i) for i in devices]
    return lax.ppermute(block, axis, route)


def row_round(states, weight):
    sent = (weight * states[0], weight * states[1], weight * states[2], weight)
    below = passed_along((sent[0], sent[1], sent[2], sent[3]), "row", 1)
    above = passed_along((sent[0], sent[1], sent[2], sent[3]), "row", -1)
    total = below[3] + weight + above[3]
    merged = tuple(((below[i] + sent[i] + above[i]) / total for i in range(3)))
    return (merged, total / 3.0)


def col_round(states, weight):
    sent = (weight * states[0], weight * states[1], weight * states[2], weight)
    below = passed_along((sent[0], sent[1], sent[2], sent[3]), "col", 1)
    above = passed_along((sent[0], sent[1], sent[2], sent[3]), "col", -1)
    total = below[3] + weight + above[3]
    merged = tuple(((below[i] + sent[i] + above[i]) / total for i in range(3)))
    return merged


def finish(states, weight):
    after_row, mass = row_round(states, weight)
    after_col = col_round(after_row, mass)
    rounded = after_col[0].astype(jnp.bfloat16)
    whole = lax.all_gather(rounded, "fsdp", axis=2, tiled=True)
    return (after_col, whole[:, :, None])


def per_device(master, moment_one, moment_two, grads, counts, step):
    steps_f = step[0].astype(jnp.float32)
    grad_f = grads.astype(jnp.float32)
    first = 0.9 * moment_one + 0.1 * grad_f
    second = 0.95 * moment_two + 0.05 * grad_f * grad_f
    first_hat = first / (1.0 - jnp.power(jnp.float32(0.9), steps_f))
    second_hat = second / (1.0 - jnp.power(jnp.float32(0.95), steps_f))
    updated = master - 0.1 * (first_hat / (jnp.sqrt(second_hat) + 1e-08) + 0.1 * master)
    lengths = 256.0 * jnp.power(2.0, jnp.arange(counts.shape[2]).astype(jnp.float32))
    weight = jnp.sum(counts.astype(jnp.float32) * lengths, axis=-1)[:, :, None, None]
    states, copies = finish((updated, first, second), weight)
    return (states[0], states[1], states[2], copies)


def solution(mesh):
    return jax.shard_map(
        per_device,
        mesh=mesh,
        in_specs=(
            P("row", "col", "fsdp", None),
            P("row", "col", "fsdp", None),
            P("row", "col", "fsdp", None),
            P("row", "col", "fsdp", None),
            P("row", "col", None),
            P(),
        ),
        out_specs=(
            P("row", "col", "fsdp", None),
            P("row", "col", "fsdp", None),
            P("row", "col", "fsdp", None),
            P("row", "col", "fsdp", None, None),
        ),
        check_vma=False,
    )
```

profile of v0, /device:TPU:1, one launch (start us, length us, event | category | flops | bytes accessed | tf_op | source)
XLA Modules:
  0.0 321.7 jit_solution(8683162505661463940)
XLA Ops:
  7.2 1.3 multiply_reduce_fusion
  9.2 2.3 fusion.3
  11.6 6.9 %collective-permute-start.3 = (f32[1,1,24,4096]{3,2,1,0:T(8,128)S(1)}, f32[1,1,24,4096]{3,2,1,0:T(8,128)S(1)}, u32[]{:S(2)}, u32[]{:S(2)}) collective-permute-start(f32[1,1,24,4096]{3,2,1,0:T(8,128)S(1)} %get-tuple-element.7), channel_id=1, source_target_pairs={{64,0},{128,64},{192,128},{256,192},{320,256},{384,320},{448,384},... | collective-permute-start | bytes 1179656 | tf_op jit(solution)/shard_map/ppermute | solution.py:10
  19.0 3.0 collective-permute-start.9
  21.9 1.3 collective-permute-done
  23.2 2.5 collective-permute-start.8
  27.7 12.0 %collective-permute-start.6 = (f32[1,1,1,1]{3,2,1,0:T(1,128)}, f32[1,1,1,1]{3,2,1,0:T(1,128)}, u32[]{:S(2)}, u32[]{:S(2)}) collective-permute-start(f32[1,1,1,1]{3,2,1,0:T(1,128)} %div.60), channel_id=1, source_target_pairs={{56,0},{0,8},{8,16},{16,24},{24,32},{32,40},{40,48},{48,56},{57,1}... | collective-permute-start | bytes 20 | tf_op jit(solution)/shard_map/ppermute | solution.py:10
  39.7 3.2 %collective-permute-done.6 = f32[1,1,1,1]{3,2,1,0:T(1,128)} collective-permute-done((f32[1,1,1,1]{3,2,1,0:T(1,128)}, f32[1,1,1,1]{3,2,1,0:T(1,128)}, u32[]{:S(2)}, u32[]{:S(2)}) %collective-permute-start.6) | collective-permute-done | bytes 36 | tf_op jit(solution)/shard_map/ppermute | solution.py:10
  42.9 12.1 %collective-permute-start.7 = (f32[1,1,1,1]{3,2,1,0:T(1,128)}, f32[1,1,1,1]{3,2,1,0:T(1,128)}, u32[]{:S(2)}, u32[]{:S(2)}) collective-permute-start(f32[1,1,1,1]{3,2,1,0:T(1,128)} %div.60), channel_id=1, source_target_pairs={{8,0},{16,8},{24,16},{32,24},{40,32},{48,40},{56,48},{0,56},{9,1},... | collective-permute-start | bytes 20 | tf_op jit(solution)/shard_map/ppermute | solution.py:10
  56.0 4.0 %collective-permute-start.13 = (f32[1,1,24,4096]{3,2,1,0:T(8,128)S(1)}, f32[1,1,24,4096]{3,2,1,0:T(8,128)S(1)}, u32[]{:S(2)}, u32[]{:S(2)}) collective-permute-start(f32[1,1,24,4096]{3,2,1,0:T(8,128)S(1)} %get-tuple-element.6), channel_id=1, source_target_pairs={{64,0},{128,64},{192,128},{256,192},{320,256},{384,320},{448,384},... | collective-permute-start | bytes 1179656 | tf_op jit(solution)/shard_map/ppermute | solution.py:10
  60.8 13.9 %collective-permute-start.5 = (f32[1,1,24,4096]{3,2,1,0:T(8,128)S(1)}, f32[1,1,24,4096]{3,2,1,0:T(8,128)S(1)}, u32[]{:S(2)}, u32[]{:S(2)}) collective-permute-start(f32[1,1,24,4096]{3,2,1,0:T(8,128)S(1)} %divide_multiply_fusion.2), channel_id=1, source_target_pairs={{8,0},{16,8},{24,16},{32,24},{40,32},{48,40},{56,48},{0,56},{9,1},... | collective-permute-start | bytes 1179656 | tf_op jit(solution)/shard_map/ppermute | solution.py:10
  74.8 1.9 collective-permute-start.4
  76.8 14.2 %collective-permute-start.11 = (f32[1,1,24,4096]{3,2,1,0:T(8,128)S(1)}, f32[1,1,24,4096]{3,2,1,0:T(8,128)S(1)}, u32[]{:S(2)}, u32[]{:S(2)}) collective-permute-start(f32[1,1,24,4096]{3,2,1,0:T(8,128)S(1)} %divide_multiply_fusion.1), channel_id=1, source_target_pairs={{8,0},{16,8},{24,16},{32,24},{40,32},{48,40},{56,48},{0,56},{9,1},... | collective-permute-start | bytes 1179656 | tf_op jit(solution)/shard_map/ppermute | solution.py:10
  91.0 6.0 %collective-permute-start.10 = (f32[1,1,24,4096]{3,2,1,0:T(8,128)S(1)}, f32[1,1,24,4096]{3,2,1,0:T(8,128)S(1)}, u32[]{:S(2)}, u32[]{:S(2)}) collective-permute-start(f32[1,1,24,4096]{3,2,1,0:T(8,128)S(1)} %divide_multiply_fusion.1), channel_id=1, source_target_pairs={{56,0},{0,8},{8,16},{16,24},{24,32},{32,40},{40,48},{48,56},{57,1}... | collective-permute-start | bytes 1179656 | tf_op jit(solution)/shard_map/ppermute | solution.py:10
  97.0 12.0 %collective-permute-done.4 = f32[1,1,24,4096]{3,2,1,0:T(8,128)S(1)} collective-permute-done((f32[1,1,24,4096]{3,2,1,0:T(8,128)S(1)}, f32[1,1,24,4096]{3,2,1,0:T(8,128)S(1)}, u32[]{:S(2)}, u32[]{:S(2)}) %collective-permute-start.4) | collective-permute-done | bytes 393248 | tf_op jit(solution)/shard_map/ppermute | solution.py:10
  109.0 0.9 fusion.4
  110.0 12.7 %collective-permute-start.15 = (f32[1,1,24,4096]{3,2,1,0:T(8,128)S(1)}, f32[1,1,24,4096]{3,2,1,0:T(8,128)S(1)}, u32[]{:S(2)}, u32[]{:S(2)}) collective-permute-start(f32[1,1,24,4096]{3,2,1,0:T(8,128)S(1)} %divide_multiply_fusion), channel_id=1, source_target_pairs={{8,0},{16,8},{24,16},{32,24},{40,32},{48,40},{56,48},{0,56},{9,1},... | collective-permute-start | bytes 1179656 | tf_op jit(solution)/shard_map/ppermute | solution.py:10
  122.7 1.9 collective-permute-start.14
  124.6 26.9 %collective-permute-done.10 = f32[1,1,24,4096]{3,2,1,0:T(8,128)S(1)} collective-permute-done((f32[1,1,24,4096]{3,2,1,0:T(8,128)S(1)}, f32[1,1,24,4096]{3,2,1,0:T(8,128)S(1)}, u32[]{:S(2)}, u32[]{:S(2)}) %collective-permute-start.10) | collective-permute-done | bytes 393248 | tf_op jit(solution)/shard_map/ppermute | solution.py:10
  151.5 0.8 add_divide_fusion.1
  152.4 88.2 %collective-permute-done.14 = f32[1,1,24,4096]{3,2,1,0:T(8,128)S(1)} collective-permute-done((f32[1,1,24,4096]{3,2,1,0:T(8,128)S(1)}, f32[1,1,24,4096]{3,2,1,0:T(8,128)S(1)}, u32[]{:S(2)}, u32[]{:S(2)}) %collective-permute-start.14) | collective-permute-done | bytes 393248 | tf_op jit(solution)/shard_map/ppermute | solution.py:10
  240.6 0.8 add_divide_fusion
  241.4 70.8 %all-gather.2.cloned.1.call-done = bf16[1,1,192,4096]{3,2,1,0:T(8,128)(2,1)} async-done(((bf16[1,1,24,4096]{3,2,1,0:T(8,128)(2,1)}), bf16[1,1,192,4096]{3,2,1,0:T(8,128)(2,1)}) %all-gather.2.cloned.1.call-update) | async-done | bytes 1572880 | tf_op jit(solution)/shard_map/all_gather | solution.py:35
  312.2 2.7 copy.12
  (20 shorter events, 1.2 us)
Async XLA Ops:
  7.2 305.0 %all-gather.2.cloned.1.call-start = ((), (), s32[]{:S(2)}) async-start(), calls=%async_computation | async-start | bytes 1769472 | tf_op jit(solution)/shard_map/all_gather | solution.py:35
  11.6 49.1 %collective-permute-start.3 = (f32[1,1,24,4096]{3,2,1,0:T(8,128)S(1)}, f32[1,1,24,4096]{3,2,1,0:T(8,128)S(1)}, u32[]{:S(2)}, u32[]{:S(2)}) collective-permute-start(f32[1,1,24,4096]{3,2,1,0:T(8,128)S(1)} %get-tuple-element.7), channel_id=1, source_target_pairs={{64,0},{128,64},{192,128},{256,192},{320,256},{384,320},{448,384},... | collective-permute-start | bytes 1179656 | tf_op jit(solution)/shard_map/ppermute | solution.py:10
  18.4 42.3 %collective-permute-start.2 = (f32[1,1,24,4096]{3,2,1,0:T(8,128)S(1)}, f32[1,1,24,4096]{3,2,1,0:T(8,128)S(1)}, u32[]{:S(2)}, u32[]{:S(2)}) collective-permute-start(f32[1,1,24,4096]{3,2,1,0:T(8,128)S(1)} %get-tuple-element.7), channel_id=1, source_target_pairs={{448,0},{0,64},{64,128},{128,192},{192,256},{256,320},{320,384},{3... | collective-permute-start | bytes 1179656 | tf_op jit(solution)/shard_map/ppermute | solution.py:10
  18.4 4.8 %collective-permute-start = (f32[1,1,1,1]{3,2,1,0:T(1,128)}, f32[1,1,1,1]{3,2,1,0:T(1,128)}, u32[]{:S(2)}, u32[]{:S(2)}) collective-permute-start(f32[1,1,1,1]{3,2,1,0:T(1,128)} %bitcast), channel_id=1, source_target_pairs={{448,0},{0,64},{64,128},{128,192},{192,256},{256,320},{320,384},{3... | collective-permute-start | bytes 20 | tf_op jit(solution)/shard_map/ppermute | solution.py:10
  18.4 8.6 %collective-permute-start.1 = (f32[1,1,1,1]{3,2,1,0:T(1,128)}, f32[1,1,1,1]{3,2,1,0:T(1,128)}, u32[]{:S(2)}, u32[]{:S(2)}) collective-permute-start(f32[1,1,1,1]{3,2,1,0:T(1,128)} %bitcast), channel_id=1, source_target_pairs={{64,0},{128,64},{192,128},{256,192},{320,256},{384,320},{448,384},... | collective-permute-start | bytes 20 | tf_op jit(solution)/shard_map/ppermute | solution.py:10
  19.0 55.8 %collective-permute-start.9 = (f32[1,1,24,4096]{3,2,1,0:T(8,128)S(1)}, f32[1,1,24,4096]{3,2,1,0:T(8,128)S(1)}, u32[]{:S(2)}, u32[]{:S(2)}) collective-permute-start(f32[1,1,24,4096]{3,2,1,0:T(8,128)S(1)} %get-tuple-element.8), channel_id=1, source_target_pairs={{64,0},{128,64},{192,128},{256,192},{320,256},{384,320},{448,384},... | collective-permute-start | bytes 1179656 | tf_op jit(solution)/shard_map/ppermute | solution.py:10
  23.2 53.5 %collective-permute-start.8 = (f32[1,1,24,4096]{3,2,1,0:T(8,128)S(1)}, f32[1,1,24,4096]{3,2,1,0:T(8,128)S(1)}, u32[]{:S(2)}, u32[]{:S(2)}) collective-permute-start(f32[1,1,24,4096]{3,2,1,0:T(8,128)S(1)} %get-tuple-element.8), channel_id=1, source_target_pairs={{448,0},{0,64},{64,128},{128,192},{192,256},{256,320},{320,384},{3... | collective-permute-start | bytes 1179656 | tf_op jit(solution)/shard_map/ppermute | solution.py:10
  27.7 15.2 %collective-permute-start.6 = (f32[1,1,1,1]{3,2,1,0:T(1,128)}, f32[1,1,1,1]{3,2,1,0:T(1,128)}, u32[]{:S(2)}, u32[]{:S(2)}) collective-permute-start(f32[1,1,1,1]{3,2,1,0:T(1,128)} %div.60), channel_id=1, source_target_pairs={{56,0},{0,8},{8,16},{16,24},{24,32},{32,40},{40,48},{48,56},{57,1}... | collective-permute-start | bytes 20 | tf_op jit(solution)/shard_map/ppermute | solution.py:10
  42.9 13.1 %collective-permute-start.7 = (f32[1,1,1,1]{3,2,1,0:T(1,128)}, f32[1,1,1,1]{3,2,1,0:T(1,128)}, u32[]{:S(2)}, u32[]{:S(2)}) collective-permute-start(f32[1,1,1,1]{3,2,1,0:T(1,128)} %div.60), channel_id=1, source_target_pairs={{8,0},{16,8},{24,16},{32,24},{40,32},{48,40},{56,48},{0,56},{9,1},... | collective-permute-start | bytes 20 | tf_op jit(solution)/shard_map/ppermute | solution.py:10
  56.0 53.9 %collective-permute-start.13 = (f32[1,1,24,4096]{3,2,1,0:T(8,128)S(1)}, f32[1,1,24,4096]{3,2,1,0:T(8,128)S(1)}, u32[]{:S(2)}, u32[]{:S(2)}) collective-permute-start(f32[1,1,24,4096]{3,2,1,0:T(8,128)S(1)} %get-tuple-element.6), channel_id=1, source_target_pairs={{64,0},{128,64},{192,128},{256,192},{320,256},{384,320},{448,384},... | collective-permute-start | bytes 1179656 | tf_op jit(solution)/shard_map/ppermute | solution.py:10
  60.7 49.2 %collective-permute-start.12 = (f32[1,1,24,4096]{3,2,1,0:T(8,128)S(1)}, f32[1,1,24,4096]{3,2,1,0:T(8,128)S(1)}, u32[]{:S(2)}, u32[]{:S(2)}) collective-permute-start(f32[1,1,24,4096]{3,2,1,0:T(8,128)S(1)} %get-tuple-element.6), channel_id=1, source_target_pairs={{448,0},{0,64},{64,128},{128,192},{192,256},{256,320},{320,384},{3... | collective-permute-start | bytes 1179656 | tf_op jit(solution)/shard_map/ppermute | solution.py:10
  60.8 30.2 %collective-permute-start.5 = (f32[1,1,24,4096]{3,2,1,0:T(8,128)S(1)}, f32[1,1,24,4096]{3,2,1,0:T(8,128)S(1)}, u32[]{:S(2)}, u32[]{:S(2)}) collective-permute-start(f32[1,1,24,4096]{3,2,1,0:T(8,128)S(1)} %divide_multiply_fusion.2), channel_id=1, source_target_pairs={{8,0},{16,8},{24,16},{32,24},{40,32},{48,40},{56,48},{0,56},{9,1},... | collective-permute-start | bytes 1179656 | tf_op jit(solution)/shard_map/ppermute | solution.py:10
  74.8 34.2 %collective-permute-start.4 = (f32[1,1,24,4096]{3,2,1,0:T(8,128)S(1)}, f32[1,1,24,4096]{3,2,1,0:T(8,128)S(1)}, u32[]{:S(2)}, u32[]{:S(2)}) collective-permute-start(f32[1,1,24,4096]{3,2,1,0:T(8,128)S(1)} %divide_multiply_fusion.2), channel_id=1, source_target_pairs={{56,0},{0,8},{8,16},{16,24},{24,32},{32,40},{40,48},{48,56},{57,1}... | collective-permute-start | bytes 1179656 | tf_op jit(solution)/shard_map/ppermute | solution.py:10
  76.8 47.9 %collective-permute-start.11 = (f32[1,1,24,4096]{3,2,1,0:T(8,128)S(1)}, f32[1,1,24,4096]{3,2,1,0:T(8,128)S(1)}, u32[]{:S(2)}, u32[]{:S(2)}) collective-permute-start(f32[1,1,24,4096]{3,2,1,0:T(8,128)S(1)} %divide_multiply_fusion.1), channel_id=1, source_target_pairs={{8,0},{16,8},{24,16},{32,24},{40,32},{48,40},{56,48},{0,56},{9,1},... | collective-permute-start | bytes 1179656 | tf_op jit(solution)/shard_map/ppermute | solution.py:10
  91.0 60.6 %collective-permute-start.10 = (f32[1,1,24,4096]{3,2,1,0:T(8,128)S(1)}, f32[1,1,24,4096]{3,2,1,0:T(8,128)S(1)}, u32[]{:S(2)}, u32[]{:S(2)}) collective-permute-start(f32[1,1,24,4096]{3,2,1,0:T(8,128)S(1)} %divide_multiply_fusion.1), channel_id=1, source_target_pairs={{56,0},{0,8},{8,16},{16,24},{24,32},{32,40},{40,48},{48,56},{57,1}... | collective-permute-start | bytes 1179656 | tf_op jit(solution)/shard_map/ppermute | solution.py:10
  110.0 42.4 %collective-permute-start.15 = (f32[1,1,24,4096]{3,2,1,0:T(8,128)S(1)}, f32[1,1,24,4096]{3,2,1,0:T(8,128)S(1)}, u32[]{:S(2)}, u32[]{:S(2)}) collective-permute-start(f32[1,1,24,4096]{3,2,1,0:T(8,128)S(1)} %divide_multiply_fusion), channel_id=1, source_target_pairs={{8,0},{16,8},{24,16},{32,24},{40,32},{48,40},{56,48},{0,56},{9,1},... | collective-permute-start | bytes 1179656 | tf_op jit(solution)/shard_map/ppermute | solution.py:10
  122.7 117.9 %collective-permute-start.14 = (f32[1,1,24,4096]{3,2,1,0:T(8,128)S(1)}, f32[1,1,24,4096]{3,2,1,0:T(8,128)S(1)}, u32[]{:S(2)}, u32[]{:S(2)}) collective-permute-start(f32[1,1,24,4096]{3,2,1,0:T(8,128)S(1)} %divide_multiply_fusion), channel_id=1, source_target_pairs={{56,0},{0,8},{8,16},{16,24},{24,32},{32,40},{40,48},{48,56},{57,1}... | collective-permute-start | bytes 1179656 | tf_op jit(solution)/shard_map/ppermute | solution.py:10
Sparse Core Ops, SparseCore 0:
  110.0 202.1 all-gather.1
where the time goes:
time: 323 us; the launch traced here: 322 us
  waiting for transfers between devices  203 us (63%)
  starting transfers between devices  91.6 us (28%)
  between operations  18.3 us (6%)
  other arithmetic  6.3 us (2%)
    ppermute x16, waiting for transfers between devices, passed_along(): return lax.ppermute(block, axis, route)  132 us
    ppermute x16, starting transfers between devices, passed_along(): return lax.ppermute(block, axis, route)  91.6 us
    all_gather x1, waiting for transfers between devices, finish(): whole = lax.all_gather(rounded, 'fsdp', axis=2, tiled=True)  70.8 us
  transfers between devices with their start and end apart: 17, of which 7 were waited for; matrix products, arithmetic and copies ran while one was open for 1% of the time, Pallas kernels for 0%

commit v1 on v0

v1 whole, which is shorter than its diff:
```python
import jax
import jax.numpy as jnp
from jax import lax
from jax.experimental import pallas as pl
from jax.experimental.pallas import tpu as pltpu
from jax.sharding import PartitionSpec as P

MESH = pl.DeviceIdType.MESH
X, M, V = 0, 1, 2
GROUPS = 3
CHUNKS = 9
D = 4096
HALF = D // 2
TILE = 512
SPAN = (14.0, 3.5, 3.5)
LEVELS = 32767.0


def wide(tile, columns):
    return jnp.concatenate([tile] * (columns // 128), axis=1)


def encode(value, span):
    size = jnp.maximum(jnp.abs(value) * (1.0 / span), 1e-30)
    root = lax.rsqrt(lax.rsqrt(size)) * LEVELS + 0.5
    level = jnp.minimum(root, LEVELS).astype(jnp.int32)
    return jnp.where(value < 0.0, -level, level)


def decode(code, span):
    root = code.astype(jnp.int32).astype(jnp.float32) * (1.0 / LEVELS)
    square = root * root
    return (square * span) * (root * jnp.abs(root))


def power(base, steps):
    result = jnp.full(steps.shape, 1.0, jnp.float32)
    for bit in range(11):
        factor = jnp.float32(base ** (2**bit))
        result = jnp.where((steps >> bit) & 1 == 1, result * factor, result)
    return jnp.where(steps >= 2048, 0.0, result)


SCHEDULE = (
    "A0", "A1", "B0", "A2", "A3", "B1", "A4", "B2", "A5", "A6",
    "B3", "C0", "A7", "B4", "C1", "A8", "B5", "C2", "B6", "B7",
    "B8", "G1", "G2", "C3", "G3", "C4", "G4", "C5", "G5", "C6",
    "G6", "C7", "G7", "C8",
)


def kernel(
    master, moment_one, moment_two, grads, counts, step,
    new_master, new_one, new_two, whole,
    grad_f, own, below, above, rowed, side, sent, got,
    tok, mass,
    row_send, row_recv, x_send, x_recv, z_send, z_recv, tok_send, tok_recv,
    ag_send, ag_recv,
):
    r, c, f = lax.axis_index("row"), lax.axis_index("col"), lax.axis_index("fsdp")
    nr, nc, nf = (lax.axis_size(a) for a in ("row", "col", "fsdp"))
    hi = lax.rem(c, 2)
    up, down = (lax.rem(r + 1, nr), c, f), (lax.rem(r + nr - 1, nr), c, f)
    plus, minus = lax.rem(c + 2, nc), lax.rem(c + nc - 2, nc)
    x_to = (r, hi * plus + (1 - hi) * minus, f)
    z_to = (r, c + 1 - 2 * hi, f)
    right, left = (r, c, lax.rem(f + 1, nf)), (r, c, lax.rem(f + nf - 1, nf))

    barrier = pltpu.get_barrier_semaphore()
    for other in (up, down, (r, plus, f), (r, minus, f), z_to, right, left):
        pl.semaphore_signal(barrier, 1, device_id=other, device_id_type=MESH)
    pl.semaphore_wait(barrier, 7)

    def remote(src, dst, send, recv, to):
        return pltpu.make_async_remote_copy(
            src_ref=src, dst_ref=dst, send_sem=send, recv_sem=recv, device_id=to, device_id_type=MESH
        )

    def tok_copy(i):
        src, dst, to = (
            (tok.at[0], tok.at[1], up),
            (tok.at[0], tok.at[2], down),
            (mass.at[0], mass.at[1], x_to),
            (mass.at[2], mass.at[3], z_to),
        )[i]
        return remote(src, dst, tok_send.at[i], tok_recv.at[i], to)

    def row_copy(i, q):
        dst, to = ((below, up), (above, down))[i]
        return remote(own.at[q], dst.at[q], row_send.at[i, q], row_recv.at[i, q], to)

    def x_copy(q):
        return remote(rowed.at[q], side.at[q], x_send.at[q], x_recv.at[q], x_to)

    def z_copy(q):
        return remote(sent.at[q], got.at[q], z_send.at[q], z_recv.at[q], z_to)

    def ag_copy(way, shard, g):
        at = shard * GROUPS + g
        return remote(whole.at[at], whole.at[at], ag_send.at[way, at], ag_recv.at[at], (right, left)[way])

    def each_tile(columns, body):
        def one(i, carry):
            body(pl.multiple_of(i * TILE, TILE))
            return carry

        lax.fori_loop(0, columns // TILE, one, 0)

    total = counts[0]
    for b in range(1, counts.shape[0]):
        total = total + counts[b] * (2**b)
    weight = jnp.full((8, 128), (total * 256).astype(jnp.float32), jnp.float32)
    tok[0] = weight
    tok_copy(0).start()
    tok_copy(1).start()

    def to_float(at):
        cols = pl.ds(at, TILE)
        grad_f[:, cols] = grads[:, cols].astype(jnp.float32)

    each_tile(D, to_float)

    steps = jnp.full((8, 128), step[0], jnp.int32)
    fix_one = wide(1.0 / (1.0 - power(0.9, steps)), TILE)
    fix_two = wide(1.0 / (1.0 - power(0.95, steps)), TILE)
    weight = wide(weight, TILE)
    for g in range(GROUPS):

        def adam(at, g=g):
            cols, rows = pl.ds(at, TILE), pl.ds(8 * g, 8)
            grad = grad_f[rows, cols]
            first = 0.9 * moment_one[rows, cols] + 0.1 * grad
            second = 0.95 * moment_two[rows, cols] + 0.05 * grad * grad
            old = master[rows, cols]
            move = (first * fix_one) / (jnp.sqrt(second * fix_two) + 1e-08)
            own[X * GROUPS + g, :, cols] = (old - 0.1 * (move + 0.1 * old)) * weight
            own[M * GROUPS + g, :, cols] = first * weight
            own[V * GROUPS + g, :, cols] = second * weight

        each_tile(D, adam)
        row_copy(0, g).start()
        row_copy(1, g).start()
    for q in range(GROUPS, CHUNKS):
        row_copy(0, q).start()
        row_copy(1, q).start()

    def stage_a(q):
        if q == 0:
            tok_copy(0).wait_recv()
            tok_copy(1).wait_recv()
            mass[0] = tok[0] + tok[1] + tok[2]
            tok_copy(2).start()
        row_copy(0, q).wait_recv()
        row_copy(1, q).wait_recv()

        def body(at):
            cols = pl.ds(at, TILE)
            rowed[q, :, cols] = own[q, :, cols] + below[q, :, cols] + above[q, :, cols]

        each_tile(D, body)
        x_copy(q).start()

    def stage_b(q):
        if q == 0:
            tok_copy(2).wait_recv()
            mass[2] = mass[0] + mass[1]
            tok_copy(3).start()
        x_copy(q).wait_recv()
        scale = wide(1.0 / mass[2], TILE)
        span = SPAN[q // GROUPS]

        def body(at):
            halves = []
            for start in (0, HALF):
                cols = pl.ds(pl.multiple_of(at + start, TILE), TILE)
                halves.append(encode((rowed[q, :, cols] + side[q, :, cols]) * scale, span))
            sent[q, :, pl.ds(at, TILE)] = jnp.concatenate(halves, axis=0).astype(jnp.int16)

        each_tile(HALF, body)
        z_copy(q).start()

    def stage_c(q):
        if q == 0:
            tok_copy(3).wait_recv()
        z_copy(q).wait_recv()
        back = wide(mass[3], TILE)
        scale = wide(1.0 / (mass[0] + mass[3]), TILE)
        state, g = divmod(q, GROUPS)
        out = (new_master, new_one, new_two)[state]

        def body(at):
            other = decode(got[q, :, pl.ds(at, TILE)], SPAN[state])
            halves = []
            for i, start in enumerate((0, HALF)):
                cols = pl.ds(pl.multiple_of(at + start, TILE), TILE)
                mean = (rowed[q, :, cols] + other[8 * i : 8 * i + 8] * back) * scale
                out[8 * g : 8 * g + 8, cols] = mean
                halves.append(mean)
            if state == X:
                whole[f * GROUPS + g, :, pl.ds(at, TILE)] = jnp.concatenate(halves, axis=0).astype(jnp.bfloat16)

        each_tile(HALF, body)
        if state == X:

            @pl.when(f < nf - 1)
            def _():
                ag_copy(0, f, g).start()

            @pl.when(f > 0)
            def _():
                ag_copy(1, f, g).start()

    def stage_g(k):
        for g in range(GROUPS):

            @pl.when(f >= k)
            def _():
                ag_copy(0, f - k, g).wait_recv()

                @pl.when(f < nf - 1)
                def _():
                    ag_copy(0, f - k, g).start()

            @pl.when(f + k < nf)
            def _():
                ag_copy(1, f + k, g).wait_recv()

                @pl.when(f > 0)
                def _():
                    ag_copy(1, f + k, g).start()

    for name in SCHEDULE:
        {"A": stage_a, "B": stage_b, "C": stage_c, "G": stage_g}[name[0]](int(name[1:]))

    for i in range(4):
        tok_copy(i).wait_send()
    for q in range(CHUNKS):
        row_copy(0, q).wait_send()
        row_copy(1, q).wait_send()
        x_copy(q).wait_send()
        z_copy(q).wait_send()
    for k in range(nf):
        for g in range(GROUPS):

            @pl.when((f >= k) & (f < nf - 1))
            def _():
                ag_copy(0, f - k, g).wait_send()

            @pl.when((f + k < nf) & (f > 0))
            def _():
                ag_copy(1, f + k, g).wait_send()


def per_device(master, moment_one, moment_two, grads, counts, step):
    nf = lax.axis_size("fsdp")
    rows = master.shape[2]
    vmem = pl.BlockSpec(memory_space=pltpu.VMEM)
    smem = pl.BlockSpec(memory_space=pltpu.SMEM)
    state = jax.ShapeDtypeStruct((rows, D), jnp.float32)
    wide_chunks = pltpu.VMEM((CHUNKS, 8, D), jnp.float32)
    short_chunks = pltpu.VMEM((CHUNKS, 16, HALF), jnp.int16)
    dma = pltpu.SemaphoreType.DMA
    results = pl.pallas_call(
        kernel,
        out_shape=(state, state, state, jax.ShapeDtypeStruct((nf * GROUPS, 16, HALF), jnp.bfloat16)),
        in_specs=[vmem] * 4 + [smem] * 2,
        out_specs=[vmem] * 4,
        scratch_shapes=[pltpu.VMEM((rows, D), jnp.float32)]
        + [wide_chunks] * 5
        + [short_chunks] * 2
        + [pltpu.VMEM((3, 8, 128), jnp.float32), pltpu.VMEM((4, 8, 128), jnp.float32)]
        + [dma((2, CHUNKS))] * 2
        + [dma((CHUNKS,))] * 4
        + [dma((4,))] * 2
        + [dma((2, nf * GROUPS)), dma((nf * GROUPS,))],
        compiler_params=pltpu.CompilerParams(
            collective_id=0, has_side_effects=True, vmem_limit_bytes=40 << 20
        ),
    )(
        *(a.reshape(rows, D) for a in (master, moment_one, moment_two, grads)),
        counts.reshape(counts.shape[-1]),
        step,
    )
    copies = results[3].reshape(nf * GROUPS, 2, 8, HALF).transpose(0, 2, 1, 3)
    return (
        *(a.reshape(1, 1, rows, D) for a in results[:3]),
        copies.reshape(1, 1, 1, nf * rows, D),
    )


def solution(mesh):
    split = P("row", "col", "fsdp", None)
    return jax.shard_map(
        per_device,
        mesh=mesh,
        in_specs=(split, split, split, split, P("row", "col", None), P()),
        out_specs=(split, split, split, P("row", "col", "fsdp", None, None)),
        check_vma=False,
    )
```

time: 323 us -> 119 us (0.37)
  waiting for transfers between devices: 203 us -> 0 us
  Pallas kernels: 0 us -> 109 us
  starting transfers between devices: 91.6 us -> 0 us
  between operations: 18.3 us -> 1.3 us
  other arithmetic: 6.3 us -> 0 us
  local copies, waits for them, and re-layouts: 2.7 us -> 7.94 us
    ppermute x16 -> x0, waiting for transfers between devices: 132 us -> none  [passed_along(): return lax.ppermute(block, axis, route)]
    pallas_call x0 -> x1, Pallas kernels: none -> 109 us  [per_device(): pl.pallas_call(kernel, out_shape=(state, state, state, jax.ShapeDtypeStru...]
    ppermute x16 -> x0, starting transfers between devices: 91.6 us -> none  [passed_along(): return lax.ppermute(block, axis, route)]
    all_gather x1 -> x0, waiting for transfers between devices: 70.8 us -> none  [finish(): whole = lax.all_gather(rounded, 'fsdp', axis=2, tiled=True)]
    unnamed x1 -> x14, local copies, waits for them, and re-layouts: 2.7 us -> 7.94 us
  transfers between devices with their start and end apart: 17 -> 0, of which waited for: 7 -> 0; matrix products, arithmetic and copies ran while one was open for 1% -> 0% of each run, Pallas kernels for 0% -> 0%
where the time goes in v1:
time: 119 us
  Pallas kernels  109 us (92%)
  local copies, waits for them, and re-layouts  7.94 us (7%)
  between operations  1.3 us (1%)
    pallas_call x1, Pallas kernels, per_device(): pl.pallas_call(kernel, out_shape=(state, state, state, jax.ShapeDtypeStru...  109 us
    unnamed x14, local copies, waits for them, and re-layouts  7.94 us

profile of v1, /device:TPU:1, one launch (start us, length us, event | category | flops | bytes accessed | tf_op | source)
XLA Modules:
  0.0 118.7 jit_solution(5435980349747960116)
XLA Ops:
  1.3 0.0 copy-start
  1.3 1.0 copy-done
  2.3 0.0 copy-start.1
  2.3 1.0 copy-done.1
  3.3 0.0 copy-start.2
  3.3 1.0 copy-done.2
  4.3 0.0 copy-start.3
  4.3 0.9 copy-done.3
  5.2 0.0 copy-start.4
  5.2 0.7 copy-done.4
  5.9 109.5 %shard_map.93 = (f32[24,4096]{1,0:T(8,128)S(1)}, f32[24,4096]{1,0:T(8,128)S(1)}, f32[24,4096]{1,0:T(8,128)S(1)}, bf16[24,16,2048]{2,1,0:T(8,128)(2,1)S(1)}) custom-call(f32[24,4096]{1,0:T(8,128)S(1)} %bitcast.17, f32[24,4096]{1,0:T(8,128)S(1)} %bitcast.18, f32[24,4096]{1,0:T(8,128)S(1)} %bitcast.19, bf16[24,4096]{1,0:T(8,128)(2,1)S(1)} %bitcast.20, ...), custom_call_target="tpu_custom_call" | custom-call | tf_op jit(solution)/shard_map/pallas_call | solution.py:263
  115.3 0.7 copy.15
  116.1 0.7 copy.16
  116.8 0.7 copy.17
  117.6 1.1 copy.18
Async XLA Ops:
  1.3 1.0 copy-start
  2.3 1.0 copy-start.1
  3.3 1.0 copy-start.2
  4.3 0.9 copy-start.3
  5.2 0.7 copy-start.4

commit v2 on v1

--- a/solution.py
+++ b/solution.py
@@ -52,8 +52,8 @@
 def kernel(
     master, moment_one, moment_two, grads, counts, step,
     new_master, new_one, new_two, whole,
-    grad_f, own, below, above, rowed, side, sent, got,
-    tok, mass,
+    grad_f, was, was_one, was_two, was_grad, own, below, above, rowed, side, sent, got,
+    tok, mass, load,
     row_send, row_recv, x_send, x_recv, z_send, z_recv, tok_send, tok_recv,
     ag_send, ag_recv,
 ):
@@ -69,7 +69,14 @@
     barrier = pltpu.get_barrier_semaphore()
     for other in (up, down, (r, plus, f), (r, minus, f), z_to, right, left):
         pl.semaphore_signal(barrier, 1, device_id=other, device_id_type=MESH)
-    pl.semaphore_wait(barrier, 7)
+
+    loads = [pltpu.make_async_copy(grads, was_grad, load.at[0])]
+    for g in range(GROUPS):
+        rows = pl.ds(8 * g, 8)
+        for i, (src, dst) in enumerate(((master, was), (moment_one, was_one), (moment_two, was_two))):
+            loads.append(pltpu.make_async_copy(src.at[rows], dst.at[rows], load.at[1 + 3 * g + i]))
+    for copy in loads:
+        copy.start()
 
     def remote(src, dst, send, recv, to):
         return pltpu.make_async_remote_copy(
@@ -111,12 +118,11 @@
         total = total + counts[b] * (2**b)
     weight = jnp.full((8, 128), (total * 256).astype(jnp.float32), jnp.float32)
     tok[0] = weight
-    tok_copy(0).start()
-    tok_copy(1).start()
+    loads[0].wait()
 
     def to_float(at):
         cols = pl.ds(at, TILE)
-        grad_f[:, cols] = grads[:, cols].astype(jnp.float32)
+        grad_f[:, cols] = was_grad[:, cols].astype(jnp.float32)
 
     each_tile(D, to_float)
 
@@ -125,19 +131,25 @@
     fix_two = wide(1.0 / (1.0 - power(0.95, steps)), TILE)
     weight = wide(weight, TILE)
     for g in range(GROUPS):
+        for copy in loads[1 + 3 * g : 4 + 3 * g]:
+            copy.wait()
 
         def adam(at, g=g):
             cols, rows = pl.ds(at, TILE), pl.ds(8 * g, 8)
             grad = grad_f[rows, cols]
-            first = 0.9 * moment_one[rows, cols] + 0.1 * grad
-            second = 0.95 * moment_two[rows, cols] + 0.05 * grad * grad
-            old = master[rows, cols]
+            first = 0.9 * was_one[rows, cols] + 0.1 * grad
+            second = 0.95 * was_two[rows, cols] + 0.05 * grad * grad
+            old = was[rows, cols]
             move = (first * fix_one) / (jnp.sqrt(second * fix_two) + 1e-08)
             own[X * GROUPS + g, :, cols] = (old - 0.1 * (move + 0.1 * old)) * weight
             own[M * GROUPS + g, :, cols] = first * weight
             own[V * GROUPS + g, :, cols] = second * weight
 
         each_tile(D, adam)
+        if g == 0:
+            pl.semaphore_wait(barrier, 7)
+            tok_copy(0).start()
+            tok_copy(1).start()
         row_copy(0, g).start()
         row_copy(1, g).start()
     for q in range(GROUPS, CHUNKS):
@@ -251,10 +263,19 @@
                 ag_copy(1, f + k, g).wait_send()
 
 
+def place(*refs):
+    copies = [pltpu.make_async_copy(refs[i], refs[4 + i], refs[8].at[i]) for i in range(4)]
+    for copy in copies:
+        copy.start()
+    for copy in copies:
+        copy.wait()
+
+
 def per_device(master, moment_one, moment_two, grads, counts, step):
     nf = lax.axis_size("fsdp")
     rows = master.shape[2]
     vmem = pl.BlockSpec(memory_space=pltpu.VMEM)
+    hbm = pl.BlockSpec(memory_space=pltpu.HBM)
     smem = pl.BlockSpec(memory_space=pltpu.SMEM)
     state = jax.ShapeDtypeStruct((rows, D), jnp.float32)
     wide_chunks = pltpu.VMEM((CHUNKS, 8, D), jnp.float32)
@@ -263,28 +284,37 @@
     results = pl.pallas_call(
         kernel,
         out_shape=(state, state, state, jax.ShapeDtypeStruct((nf * GROUPS, 16, HALF), jnp.bfloat16)),
-        in_specs=[vmem] * 4 + [smem] * 2,
+        in_specs=[hbm] * 4 + [smem] * 2,
         out_specs=[vmem] * 4,
-        scratch_shapes=[pltpu.VMEM((rows, D), jnp.float32)]
+        scratch_shapes=[pltpu.VMEM((rows, D), jnp.float32)] * 4
+        + [pltpu.VMEM((rows, D), jnp.bfloat16)]
         + [wide_chunks] * 5
         + [short_chunks] * 2
         + [pltpu.VMEM((3, 8, 128), jnp.float32), pltpu.VMEM((4, 8, 128), jnp.float32)]
+        + [dma((10,))]
         + [dma((2, CHUNKS))] * 2
         + [dma((CHUNKS,))] * 4
         + [dma((4,))] * 2
         + [dma((2, nf * GROUPS)), dma((nf * GROUPS,))],
         compiler_params=pltpu.CompilerParams(
-            collective_id=0, has_side_effects=True, vmem_limit_bytes=40 << 20
+            collective_id=0, has_side_effects=True, vmem_limit_bytes=60 << 20
         ),
     )(
         *(a.reshape(rows, D) for a in (master, moment_one, moment_two, grads)),
         counts.reshape(counts.shape[-1]),
         step,
     )
-    copies = results[3].reshape(nf * GROUPS, 2, 8, HALF).transpose(0, 2, 1, 3)
+    results = (*results[:3], results[3].reshape(nf * GROUPS, 2, 8, HALF).transpose(0, 2, 1, 3).reshape(nf * rows, D))
+    results = pl.pallas_call(
+        place,
+        out_shape=[jax.ShapeDtypeStruct(a.shape, a.dtype) for a in results],
+        in_specs=[vmem] * 4,
+        out_specs=[hbm] * 4,
+        scratch_shapes=[dma((4,))],
+    )(*results)
     return (
         *(a.reshape(1, 1, rows, D) for a in results[:3]),
-        copies.reshape(1, 1, 1, nf * rows, D),
+        results[3].reshape(1, 1, 1, nf * rows, D),
     )
 
 

time: 119 us -> 116 us (0.975)
  local copies, waits for them, and re-layouts: 7.94 us -> 0 us
  Pallas kernels: 109 us -> 114 us
    unnamed x14 -> x0, local copies, waits for them, and re-layouts: 7.94 us -> none
    pallas_call x0 -> x1, Pallas kernels: none -> 3.34 us  [per_device(): pl.pallas_call(place, out_shape=[jax.ShapeDtypeStruct(a.shape, a.dtype) f...]
    pallas_call x1, Pallas kernels: 109 us -> 111 us  [per_device(): pl.pallas_call(kernel, out_shape=(state, state, state, jax.ShapeDtypeStru...]
where the time goes in v2:
time: 116 us
  Pallas kernels  114 us (98%)
  between operations  1.29 us (1%)
    pallas_call x1, Pallas kernels, per_device(): pl.pallas_call(kernel, out_shape=(state, state, state, jax.ShapeDtypeStru...  111 us
    pallas_call x1, Pallas kernels, per_device(): pl.pallas_call(place, out_shape=[jax.ShapeDtypeStruct(a.shape, a.dtype) f...  3.34 us

profile of v2, /device:TPU:1, one launch (start us, length us, event | category | flops | bytes accessed | tf_op | source)
XLA Modules:
  0.0 115.7 jit_solution(12424665934176258789)
XLA Ops:
  1.3 111.1 %shard_map.93 = (f32[24,4096]{1,0:T(8,128)}, f32[24,4096]{1,0:T(8,128)}, f32[24,4096]{1,0:T(8,128)}, bf16[24,16,2048]{2,1,0:T(8,128)(2,1)}) custom-call(f32[24,4096]{1,0:T(8,128)} %bitcast.15, f32[24,4096]{1,0:T(8,128)} %bitcast.16, f32[24,4096]{1,0:T(8,128)} %bitcast.17, bf16[24,4096]{1,0:T(8,128)(2,1)} %bitcast.18, s32[8]{0:T(128)} %bitcast.19, ...), custom_call_target="tpu_custom_call" | custom-call | tf_op jit(solution)/shard_map/pallas_call | solution.py:284
  112.4 3.3 %shard_map.94 = (f32[24,4096]{1,0:T(8,128)}, f32[24,4096]{1,0:T(8,128)}, f32[24,4096]{1,0:T(8,128)}, bf16[192,4096]{1,0:T(8,128)(2,1)}) custom-call(f32[24,4096]{1,0:T(8,128)} %get-tuple-element.12.refs_0_, f32[24,4096]{1,0:T(8,128)} %get-tuple-element.13.refs_1_, f32[24,4096]{1,0:T(8,128)} %get-tuple-element.14.refs_2_, bf16[192,4096]{1,0:T(8,128)(2,1)} %bitcast.14), custom_call_target="tpu_custom_call" | custom-call | tf_op jit(solution)/shard_map/pallas_call | solution.py:308

commit v3 on v2

--- a/solution.py
+++ b/solution.py
@@ -42,18 +42,18 @@
 
 
 SCHEDULE = (
-    "A0", "A1", "B0", "A2", "A3", "B1", "A4", "B2", "A5", "A6",
-    "B3", "C0", "A7", "B4", "C1", "A8", "B5", "C2", "B6", "B7",
-    "B8", "G1", "G2", "C3", "G3", "C4", "G4", "C5", "G5", "C6",
-    "G6", "C7", "G7", "C8",
+    "Z3", "X0", "Z4", "R0", "X1", "Z5", "F0", "R1", "Z6", "X2",
+    "F1", "R2", "Z7", "X3", "F2", "R3", "G1", "Z8", "X4", "F3",
+    "R4", "G2", "X5", "F4", "R5", "G3", "X6", "F5", "R6", "G4",
+    "X7", "F6", "R7", "G5", "X8", "F7", "R8", "G6", "G7", "F8",
 )
 
 
 def kernel(
     master, moment_one, moment_two, grads, counts, step,
     new_master, new_one, new_two, whole,
-    grad_f, was, was_one, was_two, was_grad, own, below, above, rowed, side, sent, got,
-    tok, mass, load,
+    grad_f, was, was_one, was_two, was_grad, own, summed, below, above, side, sent, got,
+    tok, load,
     row_send, row_recv, x_send, x_recv, z_send, z_recv, tok_send, tok_recv,
     ag_send, ag_recv,
 ):
@@ -62,7 +62,7 @@
     hi = lax.rem(c, 2)
     up, down = (lax.rem(r + 1, nr), c, f), (lax.rem(r + nr - 1, nr), c, f)
     plus, minus = lax.rem(c + 2, nc), lax.rem(c + nc - 2, nc)
-    x_to = (r, hi * plus + (1 - hi) * minus, f)
+    x_to = (r, hi * minus + (1 - hi) * plus, f)
     z_to = (r, c + 1 - 2 * hi, f)
     right, left = (r, c, lax.rem(f + 1, nf)), (r, c, lax.rem(f + nf - 1, nf))
 
@@ -84,20 +84,15 @@
         )
 
     def tok_copy(i):
-        src, dst, to = (
-            (tok.at[0], tok.at[1], up),
-            (tok.at[0], tok.at[2], down),
-            (mass.at[0], mass.at[1], x_to),
-            (mass.at[2], mass.at[3], z_to),
-        )[i]
-        return remote(src, dst, tok_send.at[i], tok_recv.at[i], to)
+        src, dst, to = ((0, 1, z_to), (1, 2, x_to), (3, 4, up), (3, 5, down))[i]
+        return remote(tok.at[src], tok.at[dst], tok_send.at[i], tok_recv.at[i], to)
 
     def row_copy(i, q):
         dst, to = ((below, up), (above, down))[i]
-        return remote(own.at[q], dst.at[q], row_send.at[i, q], row_recv.at[i, q], to)
+        return remote(summed.at[q], dst.at[q], row_send.at[i, q], row_recv.at[i, q], to)
 
     def x_copy(q):
-        return remote(rowed.at[q], side.at[q], x_send.at[q], x_recv.at[q], x_to)
+        return remote(got.at[q], side.at[q], x_send.at[q], x_recv.at[q], x_to)
 
     def z_copy(q):
         return remote(sent.at[q], got.at[q], z_send.at[q], z_recv.at[q], z_to)
@@ -129,7 +124,23 @@
     steps = jnp.full((8, 128), step[0], jnp.int32)
     fix_one = wide(1.0 / (1.0 - power(0.9, steps)), TILE)
     fix_two = wide(1.0 / (1.0 - power(0.95, steps)), TILE)
-    weight = wide(weight, TILE)
+
+    def stage_z(q):
+        span = SPAN[q // GROUPS]
+
+        def body(at):
+            halves = []
+            for start in (0, HALF):
+                cols = pl.ds(pl.multiple_of(at + start, TILE), TILE)
+                halves.append(encode(own[q, :, cols], span))
+            sent[q, :, pl.ds(at, TILE)] = jnp.concatenate(halves, axis=0).astype(jnp.int16)
+
+        each_tile(HALF, body)
+        if q == 0:
+            pl.semaphore_wait(barrier, 7)
+            tok_copy(0).start()
+        z_copy(q).start()
+
     for g in range(GROUPS):
         for copy in loads[1 + 3 * g : 4 + 3 * g]:
             copy.wait()
@@ -141,71 +152,56 @@
             second = 0.95 * was_two[rows, cols] + 0.05 * grad * grad
             old = was[rows, cols]
             move = (first * fix_one) / (jnp.sqrt(second * fix_two) + 1e-08)
-            own[X * GROUPS + g, :, cols] = (old - 0.1 * (move + 0.1 * old)) * weight
-            own[M * GROUPS + g, :, cols] = first * weight
-            own[V * GROUPS + g, :, cols] = second * weight
+            own[X * GROUPS + g, :, cols] = old - 0.1 * (move + 0.1 * old)
+            own[M * GROUPS + g, :, cols] = first
+            own[V * GROUPS + g, :, cols] = second
 
         each_tile(D, adam)
-        if g == 0:
-            pl.semaphore_wait(barrier, 7)
-            tok_copy(0).start()
+        stage_z(g)
+
+    def stage_x(q):
+        if q == 0:
+            tok_copy(0).wait_recv()
             tok_copy(1).start()
-        row_copy(0, g).start()
-        row_copy(1, g).start()
-    for q in range(GROUPS, CHUNKS):
+        z_copy(q).wait_recv()
+        x_copy(q).start()
+
+    def stage_r(q):
+        if q == 0:
+            tok_copy(1).wait_recv()
+            tok[3] = tok[0] + tok[1] + tok[2]
+            tok_copy(2).start()
+            tok_copy(3).start()
+        x_copy(q).wait_recv()
+        here, facing, beyond = (wide(tok[i], TILE) for i in range(3))
+        span = SPAN[q // GROUPS]
+
+        def body(at):
+            one = decode(got[q, :, pl.ds(at, TILE)], span)
+            two = decode(side[q, :, pl.ds(at, TILE)], span)
+            for i, start in ((0, 0), (8, HALF)):
+                cols = pl.ds(pl.multiple_of(at + start, TILE), TILE)
+                summed[q, :, cols] = own[q, :, cols] * here + one[i : i + 8] * facing + two[i : i + 8] * beyond
+
+        each_tile(HALF, body)
         row_copy(0, q).start()
         row_copy(1, q).start()
 
-    def stage_a(q):
+    def stage_f(q):
         if q == 0:
-            tok_copy(0).wait_recv()
-            tok_copy(1).wait_recv()
-            mass[0] = tok[0] + tok[1] + tok[2]
-            tok_copy(2).start()
+            tok_copy(2).wait_recv()
+            tok_copy(3).wait_recv()
         row_copy(0, q).wait_recv()
         row_copy(1, q).wait_recv()
-
-        def body(at):
-            cols = pl.ds(at, TILE)
-            rowed[q, :, cols] = own[q, :, cols] + below[q, :, cols] + above[q, :, cols]
-
-        each_tile(D, body)
-        x_copy(q).start()
-
-    def stage_b(q):
-        if q == 0:
-            tok_copy(2).wait_recv()
-            mass[2] = mass[0] + mass[1]
-            tok_copy(3).start()
-        x_copy(q).wait_recv()
-        scale = wide(1.0 / mass[2], TILE)
-        span = SPAN[q // GROUPS]
+        scale = wide(1.0 / (tok[3] + tok[4] + tok[5]), TILE)
+        state, g = divmod(q, GROUPS)
+        out = (new_master, new_one, new_two)[state]
 
         def body(at):
             halves = []
             for start in (0, HALF):
                 cols = pl.ds(pl.multiple_of(at + start, TILE), TILE)
-                halves.append(encode((rowed[q, :, cols] + side[q, :, cols]) * scale, span))
-            sent[q, :, pl.ds(at, TILE)] = jnp.concatenate(halves, axis=0).astype(jnp.int16)
-
-        each_tile(HALF, body)
-        z_copy(q).start()
-
-    def stage_c(q):
-        if q == 0:
-            tok_copy(3).wait_recv()
-        z_copy(q).wait_recv()
-        back = wide(mass[3], TILE)
-        scale = wide(1.0 / (mass[0] + mass[3]), TILE)
-        state, g = divmod(q, GROUPS)
-        out = (new_master, new_one, new_two)[state]
-
-        def body(at):
-            other = decode(got[q, :, pl.ds(at, TILE)], SPAN[state])
-            halves = []
-            for i, start in enumerate((0, HALF)):
-                cols = pl.ds(pl.multiple_of(at + start, TILE), TILE)
-                mean = (rowed[q, :, cols] + other[8 * i : 8 * i + 8] * back) * scale
+                mean = (summed[q, :, cols] + below[q, :, cols] + above[q, :, cols]) * scale
                 out[8 * g : 8 * g + 8, cols] = mean
                 halves.append(mean)
             if state == X:
@@ -241,8 +237,9 @@
                 def _():
                     ag_copy(1, f + k, g).start()
 
+    stages = dict(Z=stage_z, X=stage_x, R=stage_r, F=stage_f, G=stage_g)
     for name in SCHEDULE:
-        {"A": stage_a, "B": stage_b, "C": stage_c, "G": stage_g}[name[0]](int(name[1:]))
+        stages[name[0]](int(name[1:]))
 
     for i in range(4):
         tok_copy(i).wait_send()
@@ -288,9 +285,9 @@
         out_specs=[vmem] * 4,
         scratch_shapes=[pltpu.VMEM((rows, D), jnp.float32)] * 4
         + [pltpu.VMEM((rows, D), jnp.bfloat16)]
-        + [wide_chunks] * 5
-        + [short_chunks] * 2
-        + [pltpu.VMEM((3, 8, 128), jnp.float32), pltpu.VMEM((4, 8, 128), jnp.float32)]
+        + [wide_chunks] * 4
+        + [short_chunks] * 3
+        + [pltpu.VMEM((6, 8, 128), jnp.float32)]
         + [dma((10,))]
         + [dma((2, CHUNKS))] * 2
         + [dma((CHUNKS,))] * 4

time: 116 us -> 109 us (0.940)
  Pallas kernels: 114 us -> 108 us
    pallas_call x1, Pallas kernels: 111 us -> 104 us  [per_device(): pl.pallas_call(kernel, out_shape=(state, state, state, jax.ShapeDtypeStru...]
where the time goes in v3:
time: 109 us
  Pallas kernels  108 us (99%)
  between operations  1.29 us (1%)
    pallas_call x1, Pallas kernels, per_device(): pl.pallas_call(kernel, out_shape=(state, state, state, jax.ShapeDtypeStru...  104 us
    pallas_call x1, Pallas kernels, per_device(): pl.pallas_call(place, out_shape=[jax.ShapeDtypeStruct(a.shape, a.dtype) f...  3.34 us

profile of v3, /device:TPU:1, one launch (start us, length us, event | category | flops | bytes accessed | tf_op | source)
XLA Modules:
  0.0 108.9 jit_solution(616374715837441408)
XLA Ops:
  1.3 104.3 %shard_map.93 = (f32[24,4096]{1,0:T(8,128)}, f32[24,4096]{1,0:T(8,128)}, f32[24,4096]{1,0:T(8,128)}, bf16[24,16,2048]{2,1,0:T(8,128)(2,1)}) custom-call(f32[24,4096]{1,0:T(8,128)} %bitcast.15, f32[24,4096]{1,0:T(8,128)} %bitcast.16, f32[24,4096]{1,0:T(8,128)} %bitcast.17, bf16[24,4096]{1,0:T(8,128)(2,1)} %bitcast.18, s32[8]{0:T(128)} %bitcast.19, ...), custom_call_target="tpu_custom_call" | custom-call | tf_op jit(solution)/shard_map/pallas_call | solution.py:281
  105.6 3.3 %shard_map.94 = (f32[24,4096]{1,0:T(8,128)}, f32[24,4096]{1,0:T(8,128)}, f32[24,4096]{1,0:T(8,128)}, bf16[192,4096]{1,0:T(8,128)(2,1)}) custom-call(f32[24,4096]{1,0:T(8,128)} %get-tuple-element.12.refs_0_, f32[24,4096]{1,0:T(8,128)} %get-tuple-element.13.refs_1_, f32[24,4096]{1,0:T(8,128)} %get-tuple-element.14.refs_2_, bf16[192,4096]{1,0:T(8,128)(2,1)} %bitcast.14), custom_call_target="tpu_custom_call" | custom-call | tf_op jit(solution)/shard_map/pallas_call | solution.py:305

commit v4 on v3

--- a/solution.py
+++ b/solution.py
@@ -42,16 +42,17 @@
 
 
 SCHEDULE = (
-    "Z3", "X0", "Z4", "R0", "X1", "Z5", "F0", "R1", "Z6", "X2",
-    "F1", "R2", "Z7", "X3", "F2", "R3", "G1", "Z8", "X4", "F3",
-    "R4", "G2", "X5", "F4", "R5", "G3", "X6", "F5", "R6", "G4",
-    "X7", "F6", "R7", "G5", "X8", "F7", "R8", "G6", "G7", "F8",
+    "Z3", "X0", "Z4", "R0", "X1", "Z5", "F0", "R1", "X2", "Z6",
+    "F1", "R2", "Z7", "F2", "X3", "Z8", "R3", "X4", "F3", "R4",
+    "X5", "G1", "F4", "R5", "X6", "G2", "F5", "R6", "X7", "G3",
+    "F6", "R7", "X8", "G4", "F7", "R8", "G5", "F8", "G6", "G7",
 )
 
 
 def kernel(
     master, moment_one, moment_two, grads, counts, step,
-    new_master, new_one, new_two, whole,
+    out_master, out_one, out_two, out_whole,
+    new_master, new_one, new_two, whole, out_send, whole_send,
     grad_f, was, was_one, was_two, was_grad, own, summed, below, above, side, sent, got,
     tok, load,
     row_send, row_recv, x_send, x_recv, z_send, z_recv, tok_send, tok_recv,
@@ -101,6 +102,16 @@
         at = shard * GROUPS + g
         return remote(whole.at[at], whole.at[at], ag_send.at[way, at], ag_recv.at[at], (right, left)[way])
 
+    def out_copy(q):
+        state, g = divmod(q, GROUPS)
+        rows = pl.ds(8 * g, 8)
+        src, dst = ((new_master, out_master), (new_one, out_one), (new_two, out_two))[state]
+        return pltpu.make_async_copy(src.at[rows], dst.at[rows], out_send.at[q])
+
+    def whole_copy(shard, g):
+        at = shard * GROUPS + g
+        return pltpu.make_async_copy(whole.at[at], out_whole.at[at], whole_send.at[at])
+
     def each_tile(columns, body):
         def one(i, carry):
             body(pl.multiple_of(i * TILE, TILE))
@@ -208,7 +219,9 @@
                 whole[f * GROUPS + g, :, pl.ds(at, TILE)] = jnp.concatenate(halves, axis=0).astype(jnp.bfloat16)
 
         each_tile(HALF, body)
+        out_copy(q).start()
         if state == X:
+            whole_copy(f, g).start()
 
             @pl.when(f < nf - 1)
             def _():
@@ -224,6 +237,7 @@
             @pl.when(f >= k)
             def _():
                 ag_copy(0, f - k, g).wait_recv()
+                whole_copy(f - k, g).start()
 
                 @pl.when(f < nf - 1)
                 def _():
@@ -232,6 +246,7 @@
             @pl.when(f + k < nf)
             def _():
                 ag_copy(1, f + k, g).wait_recv()
+                whole_copy(f + k, g).start()
 
                 @pl.when(f > 0)
                 def _():
@@ -241,6 +256,11 @@
     for name in SCHEDULE:
         stages[name[0]](int(name[1:]))
 
+    for q in range(CHUNKS):
+        out_copy(q).wait()
+    for shard in range(nf):
+        for g in range(GROUPS):
+            whole_copy(shard, g).wait()
     for i in range(4):
         tok_copy(i).wait_send()
     for q in range(CHUNKS):
@@ -261,10 +281,21 @@
 
 
 def place(*refs):
-    copies = [pltpu.make_async_copy(refs[i], refs[4 + i], refs[8].at[i]) for i in range(4)]
-    for copy in copies:
+    sources, targets, held, (come, go) = refs[:4], refs[4:8], refs[8:12], refs[12:]
+    pieces = [(i, 0, ref.shape[0]) for i, ref in enumerate(sources[:3])]
+    rows = sources[3].shape[0] // 4
+    pieces += [(3, rows * k, rows) for k in range(4)]
+    loads, stores = [], []
+    for n, (i, first, count) in enumerate(pieces):
+        rows = pl.ds(first, count)
+        loads.append(pltpu.make_async_copy(sources[i].at[rows], held[i].at[rows], come.at[n]))
+        stores.append(pltpu.make_async_copy(held[i].at[rows], targets[i].at[rows], go.at[n]))
+    for copy in loads:
         copy.start()
-    for copy in copies:
+    for load, store in zip(loads, stores):
+        load.wait()
+        store.start()
+    for copy in stores:
         copy.wait()
 
 
@@ -282,8 +313,10 @@
         kernel,
         out_shape=(state, state, state, jax.ShapeDtypeStruct((nf * GROUPS, 16, HALF), jnp.bfloat16)),
         in_specs=[hbm] * 4 + [smem] * 2,
-        out_specs=[vmem] * 4,
-        scratch_shapes=[pltpu.VMEM((rows, D), jnp.float32)] * 4
+        out_specs=[hbm] * 4,
+        scratch_shapes=[pltpu.VMEM((rows, D), jnp.float32)] * 3
+        + [pltpu.VMEM((nf * GROUPS, 16, HALF), jnp.bfloat16), dma((CHUNKS,)), dma((nf * GROUPS,))]
+        + [pltpu.VMEM((rows, D), jnp.float32)] * 4
         + [pltpu.VMEM((rows, D), jnp.bfloat16)]
         + [wide_chunks] * 4
         + [short_chunks] * 3
@@ -305,9 +338,10 @@
     results = pl.pallas_call(
         place,
         out_shape=[jax.ShapeDtypeStruct(a.shape, a.dtype) for a in results],
-        in_specs=[vmem] * 4,
+        in_specs=[hbm] * 4,
         out_specs=[hbm] * 4,
-        scratch_shapes=[dma((4,))],
+        scratch_shapes=[pltpu.VMEM(a.shape, a.dtype) for a in results] + [dma((7,))] * 2,
+        compiler_params=pltpu.CompilerParams(vmem_limit_bytes=60 << 20),
     )(*results)
     return (
         *(a.reshape(1, 1, rows, D) for a in results[:3]),

time: 109 us -> 105 us (0.963)
  Pallas kernels: 108 us -> 103 us
    pallas_call x1, Pallas kernels: 104 us -> 100 us  [per_device(): pl.pallas_call(kernel, out_shape=(state, state, state, jax.ShapeDtypeStru...]
where the time goes in v4:
time: 105 us; the launch traced here: 104 us
  Pallas kernels  103 us (98%)
  between operations  1.29 us (1%)
    pallas_call x1, Pallas kernels, per_device(): pl.pallas_call(kernel, out_shape=(state, state, state, jax.ShapeDtypeStru...  100 us
    pallas_call x1, Pallas kernels, per_device(): pl.pallas_call(place, out_shape=[jax.ShapeDtypeStruct(a.shape, a.dtype) f...  2.64 us

profile of v4, /device:TPU:1, one launch (start us, length us, event | category | flops | bytes accessed | tf_op | source)
XLA Modules:
  0.0 104.4 jit_solution(15823633929630968349)
XLA Ops:
  1.3 100.5 %shard_map.93 = (f32[24,4096]{1,0:T(8,128)}, f32[24,4096]{1,0:T(8,128)}, f32[24,4096]{1,0:T(8,128)}, bf16[24,16,2048]{2,1,0:T(8,128)(2,1)}) custom-call(f32[24,4096]{1,0:T(8,128)} %bitcast.15, f32[24,4096]{1,0:T(8,128)} %bitcast.16, f32[24,4096]{1,0:T(8,128)} %bitcast.17, bf16[24,4096]{1,0:T(8,128)(2,1)} %bitcast.18, s32[8]{0:T(128)} %bitcast.19, ...), custom_call_target="tpu_custom_call" | custom-call | tf_op jit(solution)/shard_map/pallas_call | solution.py:312
  101.8 2.6 %shard_map.94 = (f32[24,4096]{1,0:T(8,128)}, f32[24,4096]{1,0:T(8,128)}, f32[24,4096]{1,0:T(8,128)}, bf16[192,4096]{1,0:T(8,128)(2,1)}) custom-call(f32[24,4096]{1,0:T(8,128)} %get-tuple-element.12.refs_0_, f32[24,4096]{1,0:T(8,128)} %get-tuple-element.13.refs_1_, f32[24,4096]{1,0:T(8,128)} %get-tuple-element.14.refs_2_, bf16[192,4096]{1,0:T(8,128)(2,1)} %bitcast.14), custom_call_target="tpu_custom_call" | custom-call | tf_op jit(solution)/shard_map/pallas_call | solution.py:338

commit v5 on v4

--- a/solution.py
+++ b/solution.py
@@ -42,10 +42,10 @@
 
 
 SCHEDULE = (
-    "Z3", "X0", "Z4", "R0", "X1", "Z5", "F0", "R1", "X2", "Z6",
-    "F1", "R2", "Z7", "F2", "X3", "Z8", "R3", "X4", "F3", "R4",
-    "X5", "G1", "F4", "R5", "X6", "G2", "F5", "R6", "X7", "G3",
-    "F6", "R7", "X8", "G4", "F7", "R8", "G5", "F8", "G6", "G7",
+    "Z3", "X0", "Z4", "R0", "X1", "F0", "Z5", "R1", "X2", "Z6",
+    "F1", "Z7", "R2", "F2", "X3", "Z8", "R3", "X4", "F3", "R4",
+    "X5", "G1", "F4", "R5", "X6", "G2", "G3", "F5", "R6", "X7",
+    "G4", "F6", "R7", "X8", "G5", "F7", "R8", "G6", "F8", "G7",
 )
 
 

time: 105 us -> 104 us (level)
  no operation moved by 1% of the time
where the time goes in v5:
time: 104 us
  Pallas kernels  103 us (99%)
  between operations  1.29 us (1%)
    pallas_call x1, Pallas kernels, per_device(): pl.pallas_call(kernel, out_shape=(state, state, state, jax.ShapeDtypeStru...  100 us
    pallas_call x1, Pallas kernels, per_device(): pl.pallas_call(place, out_shape=[jax.ShapeDtypeStruct(a.shape, a.dtype) f...  2.64 us

profile of v5, /device:TPU:1, one launch (start us, length us, event | category | flops | bytes accessed | tf_op | source)
XLA Modules:
  0.0 103.9 jit_solution(6514300513134264753)
XLA Ops:
  1.3 100.0 %shard_map.93 = (f32[24,4096]{1,0:T(8,128)}, f32[24,4096]{1,0:T(8,128)}, f32[24,4096]{1,0:T(8,128)}, bf16[24,16,2048]{2,1,0:T(8,128)(2,1)}) custom-call(f32[24,4096]{1,0:T(8,128)} %bitcast.15, f32[24,4096]{1,0:T(8,128)} %bitcast.16, f32[24,4096]{1,0:T(8,128)} %bitcast.17, bf16[24,4096]{1,0:T(8,128)(2,1)} %bitcast.18, s32[8]{0:T(128)} %bitcast.19, ...), custom_call_target="tpu_custom_call" | custom-call | tf_op jit(solution)/shard_map/pallas_call | solution.py:312
  101.3 2.6 %shard_map.94 = (f32[24,4096]{1,0:T(8,128)}, f32[24,4096]{1,0:T(8,128)}, f32[24,4096]{1,0:T(8,128)}, bf16[192,4096]{1,0:T(8,128)(2,1)}) custom-call(f32[24,4096]{1,0:T(8,128)} %get-tuple-element.12.refs_0_, f32[24,4096]{1,0:T(8,128)} %get-tuple-element.13.refs_1_, f32[24,4096]{1,0:T(8,128)} %get-tuple-element.14.refs_2_, bf16[192,4096]{1,0:T(8,128)(2,1)} %bitcast.14), custom_call_target="tpu_custom_call" | custom-call | tf_op jit(solution)/shard_map/pallas_call | solution.py:338
